TPU v7x, 32 devices: a whole 2x2x4 slice. The times are simulated.
32 devices in a mesh: row: 4 (over y, x), col: 8 (over z, core).
Axes of the slice: x: 2, y: 2, z: 4, core: 2. Of those that a mesh axis runs over, the one named last changes fastest.
Arguments:
- fingerprints: bfloat16 [8192, 1024], P(('row', 'col')), as said below
- probes: bfloat16 [8192, 256], P(('row', 'col')), may hold values from -6 to 6
Outputs:
- image: float32 [8192, 256], P(('row', 'col'))
Inputs may be any that keep to these rules, and one draw needn't show every extreme that they name: `fingerprints`: every entry is positive.
All inputs are finite; a program needn't handle non-finite values.
Results may differ from a plain program's by a relative error of at most 0.0031.
Values may be sent and summed in bfloat16 or wider, within the bound.
A program may use at most 64 MiB of HBM per device.

v0:
```python
import math

import jax
import jax.numpy as jnp
from jax import lax
from jax.sharding import PartitionSpec as P


def squares(rows_now):
    values = rows_now.astype(jnp.float32)
    return jnp.sum(values * values, axis=1)


def tanimoto(first_rows, second_rows, first_sq, second_sq):
    inner = lax.dot_general(
        first_rows, second_rows, (((1,), (1,)), ((), ())), preferred_element_type=jnp.float32
    )
    kernel = inner / (first_sq[:, None] + second_sq[None, :] - inner)
    return kernel.astype(jnp.bfloat16)


def per_device(fingerprints, probes):
    molecules = fingerprints.shape[0] * lax.axis_size("row") * lax.axis_size("col")
    factor = 1.0 / math.sqrt(molecules)
    column_rows, column_probes = (
        lax.all_gather(fingerprints, "row", axis=0, tiled=True),
        lax.all_gather(probes, "row", axis=0, tiled=True),
    )
    column_sq = squares(column_rows)
    shard_rows = lax.all_gather(fingerprints, "col", axis=0, tiled=True)
    kernel = tanimoto(shard_rows, column_rows, squares(shard_rows), column_sq)
    partial_value = jnp.dot(kernel, column_probes, preferred_element_type=jnp.float32)
    owned = lax.psum_scatter(partial_value, "col", scatter_dimension=0, tiled=True)
    return owned * factor


def solution(mesh):
    return jax.shard_map(
        per_device,
        mesh=mesh,
        in_specs=(P(("row", "col"), None), P(("row", "col"), None)),
        out_specs=P(("row", "col"), None),
        check_vma=False,
    )
```

profile of v0, /device:TPU:0, one launch (start us, length us, event | category | flops | bytes accessed | tf_op | source)
XLA Modules:
  0.0 151.5 jit_solution(15270870452908466009)
XLA Ops:
  6.5 0.0 all-gather.5.cloned.1.call-start
  6.5 0.7 all-gather.5.cloned.1.call-update
  7.3 0.0 all-gather.3.cloned.1.call-start
  7.3 0.7 all-gather.3.cloned.1.call-update
  8.0 0.0 reduce-scatter.2.cloned.1.call-start
  8.1 11.8 %all_gather.11 = bf16[1024,256]{1,0:T(8,128)(2,1)S(1)} all-gather(bf16[256,256]{1,0:T(8,128)(2,1)} %param.3), channel_id=1, replica_groups=mesh['row'=4,'col'=8] {'row'}, dimensions={0}, use_global_device_ids=true | all-gather | bytes 655360 | tf_op jit(solution)/shard_map/all_gather | solution.py:27
  19.9 27.4 %all-gather.5.cloned.1.call-done = bf16[1024,1024]{1,0:T(8,128)(2,1)} async-done(((bf16[256,1024]{1,0:T(8,128)(2,1)}), bf16[1024,1024]{1,0:T(8,128)(2,1)}) %all-gather.5.cloned.1.call-update) | async-done | bytes 2097168 | tf_op jit(solution)/shard_map/all_gather | solution.py:26
  47.2 0.0 copy-start
  47.2 2.2 %multiply_reduce_fusion.1 = f32[1024]{0:T(1024)S(1)} fusion(bf16[1024,1024]{1,0:T(8,128)(2,1)} %all-gather.5.cloned.1.call-done), kind=kLoop, calls=%fused_computation.3 | loop fusion | flops 3144704 | bytes 2101248 | tf_op jit(solution)/shard_map/reduce_sum | solution.py:11
  49.5 46.6 %all-gather.3.cloned.1.call-done = bf16[2048,1024]{1,0:T(8,128)(2,1)} async-done(((bf16[256,1024]{1,0:T(8,128)(2,1)}), bf16[2048,1024]{1,0:T(8,128)(2,1)}) %all-gather.3.cloned.1.call-update) | async-done | bytes 4194320 | tf_op jit(solution)/shard_map/all_gather | solution.py:30
  96.0 3.1 %multiply_reduce_fusion = f32[2048]{0:T(1024)S(1)} fusion(bf16[2048,1024]{1,0:T(8,128)(2,1)} %all-gather.3.cloned.1.call-done), kind=kLoop, calls=%fused_computation.2 | loop fusion | flops 6289408 | bytes 4202496 | tf_op jit(solution)/shard_map/reduce_sum | solution.py:11
  99.1 0.0 copy-done
  99.1 9.4 %fusion.1 = f32[2048,256]{1,0:T(8,128)} fusion(bf16[1024,256]{1,0:T(8,128)(2,1)S(1)} %all_gather.11, f32[1024]{0:T(1024)S(1)} %multiply_reduce_fusion.1, f32[2048]{0:T(1024)S(1)} %multiply_reduce_fusion, bf16[2048,1024]{1,0:T(8,128)(2,1)} %all-gather.3.cloned.1.call-done, bf16[1024,1024]{1,0:T(8,128)(2,1)S(1)} %copy-done), kind=kOutput, calls=%fused_computation.4 | convolution fusion | flops 5377097728 | bytes 8925184 | tf_op jit(solution)/shard_map/dot_general | solution.py:32
  108.5 0.0 reduce-scatter.2.cloned.1.call-update
  108.5 34.8 %reduce-scatter.2.cloned.1.call-done = f32[256,256]{1,0:T(8,128)} async-done(((f32[2048,256]{1,0:T(8,128)}), f32[256,256]{1,0:T(8,128)}) %reduce-scatter.2.cloned.1.call-update) | async-done | bytes 262160 | tf_op jit(solution)/shard_map/reduce_scatter | solution.py:33
  143.3 1.7 %broadcast_multiply_fusion = f32[256,256]{1,0:T(8,128)} fusion(f32[256,256]{1,0:T(8,128)} %reduce-scatter.2.cloned.1.call-done), kind=kLoop, calls=%fused_computation.5 | loop fusion | flops 65536 | bytes 524288 | tf_op jit(solution)/shard_map/mul | solution.py:34
Async XLA Ops:
  6.5 40.7 %all-gather.5.cloned.1.call-start = ((), (), s32[]{:S(2)}) async-start(), calls=%async_computation.2 | async-start | bytes 2621440 | tf_op jit(solution)/shard_map/all_gather | solution.py:26
  7.3 88.8 %all-gather.3.cloned.1.call-start = ((), (), s32[]{:S(2)}) async-start(), calls=%async_computation.1 | async-start | bytes 4718592 | tf_op jit(solution)/shard_map/all_gather | solution.py:30
  8.0 135.3 %reduce-scatter.2.cloned.1.call-start = ((), (), s32[]{:S(2)}) async-start(), calls=%async_computation.3 | async-start | bytes 2359296 | tf_op jit(solution)/shard_map/reduce_scatter | solution.py:33
  47.2 51.9 %copy-start = (bf16[1024,1024]{1,0:T(8,128)(2,1)S(1)}, bf16[1024,1024]{1,0:T(8,128)(2,1)}, u32[]{:S(2)}) copy-start(bf16[1024,1024]{1,0:T(8,128)(2,1)} %all-gather.5.cloned.1.call-done) | copy-start | bytes 6291460
Sparse Core Ops, SparseCore 0:
  9.2 38.0 all-gather.4
  48.8 47.1 all-gather.2
  108.7 34.5 reduce-scatter.1
where the time goes:
time: 152 us; the launch traced here: 151 us
  waiting for transfers between devices  110 us (72%)
  between operations  13.1 us (9%)
  blocking collectives  11.8 us (8%)
  matrix products  9.4 us (6%)
  other arithmetic  6.96 us (5%)
    all_gather x1, waiting for transfers between devices, per_device(): shard_rows = lax.all_gather(fingerprints, 'col', axis=0, tiled=True)  46.6 us
    reduce_scatter x1, waiting for transfers between devices, per_device(): lax.psum_scatter(partial_value, 'col', scatter_dimension=0, tiled=True)  34.8 us
    all_gather x1, waiting for transfers between devices, per_device(): lax.all_gather(fingerprints, 'row', axis=0, tiled=True)  27.4 us
    all_gather x1, blocking collectives, per_device(): lax.all_gather(probes, 'row', axis=0, tiled=True)  11.8 us
    dot_general x1, matrix products, per_device(): jnp.dot(kernel, column_probes, preferred_element_type=jnp.float32)  9.4 us
    reduce_sum x2, other arithmetic, squares(): return jnp.sum(values * values, axis=1)  5.29 us
  transfers between devices with their start and end apart: 3, of which 3 were waited for; matrix products, arithmetic and copies ran while one was open for 1% of the time, Pallas kernels for 0%

commit v1 on v0

v1 whole, which is shorter than its diff:
```python
import functools
import math

import jax
import jax.numpy as jnp
from jax import lax
from jax.experimental import pallas as pl
from jax.experimental.pallas import tpu as pltpu
from jax.sharding import PartitionSpec as P

MESH = pl.DeviceIdType.MESH
SENT = jnp.float32


def flip(index, pattern, size):
    result, weight = 0, 1
    while weight < size:
        result = result + weight * ((index // weight + pattern // weight) % 2)
        weight *= 2
    return result


def kernel(n_row, n_chip, factor, fp, pr, out, slab, cols, cpr, part, other, stage, ret, sq_first, sq_second,
           z_send, z_recv, s_send, s_recv, f_send, f_recv, p_send, p_recv, o_send, o_recv, r_send, r_recv):
    rows = fp.shape[0]
    row, col = lax.axis_index("row"), lax.axis_index("col")
    chip, core = col // 2, col % 2
    twin = col + 1 - 2 * core
    mine = pl.ds(pl.multiple_of(core * rows, rows), rows)
    others = pl.ds(pl.multiple_of((1 - core) * rows, rows), rows)

    def remote(src, dst, send, recv, where):
        return pltpu.make_async_remote_copy(
            src_ref=src, dst_ref=dst, send_sem=send, recv_sem=recv, device_id=where, device_id_type=MESH
        )

    def along(s, way, chip_to):
        return remote(slab.at[s, mine], slab.at[s, mine], z_send.at[way, s], z_recv.at[s], (row, 2 * chip_to + core))

    def to_twin(s, half):
        return remote(slab.at[s, half], slab.at[s, half], s_send.at[s], s_recv.at[s], (row, twin))

    def rows_to(p):
        peer = flip(row, p, n_row)
        return (
            remote(fp, cols.at[row], f_send.at[p], f_recv.at[p], (peer, col)),
            remote(pr, cpr.at[row], p_send.at[p], p_recv.at[p], (peer, col)),
        )

    def rows_from(p):
        peer = flip(row, p, n_row)
        return (
            remote(fp, cols.at[peer], f_send.at[p], f_recv.at[p], (peer, col)),
            remote(pr, cpr.at[peer], p_send.at[p], p_recv.at[p], (peer, col)),
        )

    def partial_to_twin(s):
        return remote(part.at[s, others], other.at[s], o_send.at[s], o_recv.at[s], (row, twin))

    def result_to(s):
        return remote(stage.at[s], ret.at[chip], r_send.at[s], r_recv.at[chip], (row, 2 * s + core))

    def result_from(s):
        return remote(stage.at[s], ret.at[s], r_send.at[s], r_recv.at[s], (row, 2 * s + core))

    def each(low, high, body):
        def step(i, carry):
            body(i)
            return carry
        lax.fori_loop(low, high, step, 0)

    barrier = pltpu.get_barrier_semaphore()

    def greet(where):
        pl.semaphore_signal(barrier, inc=1, device_id=where, device_id_type=MESH)

    each(1, n_row, lambda p: greet((flip(row, p, n_row), col)))
    each(1, n_chip, lambda d: greet((row, 2 * ((chip + d) % n_chip) + core)))
    greet((row, twin))
    slab[chip, mine] = fp[...]
    cols[row] = fp[...]
    cpr[row] = pr[...]
    pl.semaphore_wait(barrier, n_row - 1 + n_chip - 1 + 1)

    @pl.when(chip + 1 < n_chip)
    def _():
        along(chip, 0, chip + 1).start()

    @pl.when(chip > 0)
    def _():
        along(chip, 1, chip - 1).start()

    to_twin(chip, mine).start()

    def start_rows(p):
        for copy in rows_to(p):
            copy.start()
    each(1, n_row, start_rows)

    def prepare_first(s):
        values = slab[s].astype(jnp.float32)
        sq_first[s] = jnp.broadcast_to(jnp.sum(values * values, axis=1, keepdims=True), sq_first.shape[1:])

    def prepare_second(r):
        values = cols[r].astype(jnp.float32)
        total = jnp.broadcast_to(jnp.sum(values * values, axis=1, keepdims=True), (rows, 128))
        sq_second[r] = total.T[:8]

    def tile(s, r):
        inner = lax.dot_general(slab[s], cols[r], (((1,), (1,)), ((), ())), preferred_element_type=jnp.float32)
        value = inner / (sq_first[s][:, :1] + sq_second[r][:1] - inner)
        part[s] += jnp.dot(value.astype(jnp.bfloat16), cpr[r], preferred_element_type=jnp.float32)

    part[...] = jnp.zeros_like(part)
    prepare_second(row)
    to_twin(chip, others).wait_recv()
    prepare_first(chip)
    tile(chip, row)

    def receive(d, onward):
        @pl.when(chip - d >= 0)
        def _():
            along(chip - d, 0, chip).wait_recv()
            if onward:
                @pl.when(chip + 1 < n_chip)
                def _():
                    along(chip - d, 0, chip + 1).start()
            to_twin(chip - d, mine).start()

        @pl.when(chip + d < n_chip)
        def _():
            along(chip + d, 1, chip).wait_recv()
            if onward:
                @pl.when(chip > 0)
                def _():
                    along(chip + d, 1, chip - 1).start()
            to_twin(chip + d, mine).start()

    def both_sides(d, body):
        def side(k):
            s = chip + d * (2 * k - 1)

            @pl.when((s >= 0) & (s < n_chip))
            def _():
                body(s)
        each(0, 2, side)

    def take(s):
        to_twin(s, others).wait_recv()
        prepare_first(s)

    def middle(d):
        receive(d, True)

        def body(s):
            take(s)
            tile(s, row)
        both_sides(d, body)
    each(1, n_chip - 1, middle)

    last = n_chip - 1

    def near(body):
        def check(s):
            @pl.when((s - chip < last) & (chip - s < last))
            def _():
                body(s)
        each(0, n_chip, check)

    def row_step(p):
        for copy in rows_from(p):
            copy.wait_recv()
        peer = flip(row, p, n_row)
        prepare_second(peer)
        near(lambda s: tile(s, peer))
    each(1, n_row, row_step)

    def hand_on(s):
        partial_to_twin(s).wait_recv()

        @pl.when(s != chip)
        def _():
            stage[s] = (part[s, mine] + other[s]).astype(SENT)
            result_to(s).start()

    near(lambda s: partial_to_twin(s).start())
    near(hand_on)

    receive(last, False)

    def far(s):
        take(s)
        each(0, n_row, lambda r: tile(s, r))
        partial_to_twin(s).start()
        hand_on(s)
    both_sides(last, far)

    out[...] = part[chip, mine] + other[chip]

    def add(d):
        s = (chip + d) % n_chip
        result_from(s).wait_recv()
        out[...] += ret[s].astype(jnp.float32)
    each(1, n_chip, add)
    out[...] *= factor

    def sent(s):
        to_twin(s, mine).wait_send()
        partial_to_twin(s).wait_send()

        @pl.when((s <= chip) & (chip + 1 < n_chip))
        def _():
            along(s, 0, chip).wait_send()

        @pl.when((s >= chip) & (chip > 0))
        def _():
            along(s, 1, chip).wait_send()

        @pl.when(s != chip)
        def _():
            result_to(s).wait_send()
    each(0, n_chip, sent)

    def rows_sent(p):
        for copy in rows_to(p):
            copy.wait_send()
    each(1, n_row, rows_sent)


def per_device(fingerprints, probes):
    rows, features = fingerprints.shape
    width = probes.shape[1]
    n_row, n_chip = lax.axis_size("row"), lax.axis_size("col") // 2
    factor = 1.0 / math.sqrt(rows * n_row * n_chip * 2)
    dma = pltpu.SemaphoreType.DMA
    return pl.pallas_call(
        functools.partial(kernel, n_row, n_chip, factor),
        out_shape=jax.ShapeDtypeStruct((rows, width), jnp.float32),
        in_specs=[pl.BlockSpec(memory_space=pltpu.VMEM)] * 2,
        out_specs=pl.BlockSpec(memory_space=pltpu.VMEM),
        scratch_shapes=[
            pltpu.VMEM((n_chip, 2 * rows, features), jnp.bfloat16),
            pltpu.VMEM((n_row, rows, features), jnp.bfloat16),
            pltpu.VMEM((n_row, rows, width), jnp.bfloat16),
            pltpu.VMEM((n_chip, 2 * rows, width), jnp.float32),
            pltpu.VMEM((n_chip, rows, width), jnp.float32),
            pltpu.VMEM((n_chip, rows, width), SENT),
            pltpu.VMEM((n_chip, rows, width), SENT),
            pltpu.VMEM((n_chip, 2 * rows, 128), jnp.float32),
            pltpu.VMEM((n_row, 8, rows), jnp.float32),
            dma((2, n_chip)), dma((n_chip,)),
            dma((n_chip,)), dma((n_chip,)),
            dma((n_row,)), dma((n_row,)),
            dma((n_row,)), dma((n_row,)),
            dma((n_chip,)), dma((n_chip,)),
            dma((n_chip,)), dma((n_chip,)),
        ],
        compiler_params=pltpu.CompilerParams(
            collective_id=0, has_side_effects=True, vmem_limit_bytes=48 * 1024 * 1024
        ),
    )(fingerprints, probes)


def solution(mesh):
    return jax.shard_map(
        per_device,
        mesh=mesh,
        in_specs=(P(("row", "col"), None), P(("row", "col"), None)),
        out_specs=P(("row", "col"), None),
        check_vma=False,
    )
```

time: 152 us -> 67.1 us (0.44)
  the two profiles are of different devices: /device:TPU:0 before, /device:TPU:24 now
where the time goes in v1:
time: 67.1 us; the launch traced here: 66.9 us
  Pallas kernels  64.3 us (96%)
  local copies, waits for them, and re-layouts  2.65 us (4%)
    pallas_call x1, Pallas kernels, per_device(): pl.pallas_call(functools.partial(kernel, n_row, n_chip, factor), out_shap...  64.3 us
    unnamed x5, local copies, waits for them, and re-layouts  2.65 us

profile of v1, /device:TPU:24, one launch (start us, length us, event | category | flops | bytes accessed | tf_op | source)
XLA Modules:
  0.0 66.9 jit_solution(11529827708537595772)
XLA Ops:
  0.0 0.0 copy-start
  0.0 1.0 %copy-done = bf16[256,1024]{1,0:T(8,128)(2,1)S(1)} copy-done((bf16[256,1024]{1,0:T(8,128)(2,1)S(1)}, bf16[256,1024]{1,0:T(8,128)(2,1)}, u32[]{:S(2)}) %copy-start) | copy-done | bytes 524312
  1.0 0.0 copy-start.1
  1.0 0.9 %copy-done.1 = bf16[256,256]{1,0:T(8,128)(2,1)S(1)} copy-done((bf16[256,256]{1,0:T(8,128)(2,1)S(1)}, bf16[256,256]{1,0:T(8,128)(2,1)}, u32[]{:S(2)}) %copy-start.1) | copy-done | bytes 131096
  1.9 64.3 %shard_map.28 = f32[256,256]{1,0:T(8,128)S(1)} custom-call(bf16[256,1024]{1,0:T(8,128)(2,1)S(1)} %copy-done, bf16[256,256]{1,0:T(8,128)(2,1)S(1)} %copy-done.1), custom_call_target="tpu_custom_call" | custom-call | tf_op jit(solution)/shard_map/pallas_call | solution.py:236
  66.2 0.7 %copy.4 = f32[256,256]{1,0:T(8,128)} copy(f32[256,256]{1,0:T(8,128)S(1)} %shard_map.28) | data formatting | bytes 524288
Async XLA Ops:
  0.0 1.0 %copy-start = (bf16[256,1024]{1,0:T(8,128)(2,1)S(1)}, bf16[256,1024]{1,0:T(8,128)(2,1)}, u32[]{:S(2)}) copy-start(bf16[256,1024]{1,0:T(8,128)(2,1)} %fp.1) | copy-start | bytes 1572868
  1.0 0.9 %copy-start.1 = (bf16[256,256]{1,0:T(8,128)(2,1)S(1)}, bf16[256,256]{1,0:T(8,128)(2,1)}, u32[]{:S(2)}) copy-start(bf16[256,256]{1,0:T(8,128)(2,1)} %pr.1) | copy-start | bytes 393220

commit v2 on v1

--- a/solution.py
+++ b/solution.py
@@ -9,7 +9,8 @@
 from jax.sharding import PartitionSpec as P
 
 MESH = pl.DeviceIdType.MESH
-SENT = jnp.float32
+SENT = jnp.bfloat16
+CHUNKS = 2
 
 
 def flip(index, pattern, size):
@@ -21,12 +22,13 @@
 
 
 def kernel(n_row, n_chip, factor, fp, pr, out, slab, cols, cpr, part, other, stage, ret, sq_first, sq_second,
-           z_send, z_recv, s_send, s_recv, f_send, f_recv, p_send, p_recv, o_send, o_recv, r_send, r_recv):
+           z_send, z_recv, s_send, s_recv, f_send, f_recv, p_send, p_recv, o_send, o_recv, r_send, r_recv, l_sem):
     rows = fp.shape[0]
     row, col = lax.axis_index("row"), lax.axis_index("col")
     chip, core = col // 2, col % 2
     twin = col + 1 - 2 * core
     mine = pl.ds(pl.multiple_of(core * rows, rows), rows)
+    piece = rows // CHUNKS
     others = pl.ds(pl.multiple_of((1 - core) * rows, rows), rows)
 
     def remote(src, dst, send, recv, where):
@@ -34,11 +36,25 @@
             src_ref=src, dst_ref=dst, send_sem=send, recv_sem=recv, device_id=where, device_id_type=MESH
         )
 
-    def along(s, way, chip_to):
-        return remote(slab.at[s, mine], slab.at[s, mine], z_send.at[way, s], z_recv.at[s], (row, 2 * chip_to + core))
-
-    def to_twin(s, half):
-        return remote(slab.at[s, half], slab.at[s, half], s_send.at[s], s_recv.at[s], (row, twin))
+    def chunk(of, h):
+        return pl.ds(pl.multiple_of(of * rows + h * piece, piece), piece)
+
+    def along(s, way, chip_to, h):
+        place = slab.at[s, chunk(core, h)]
+        return remote(place, place, z_send.at[way, s, h], z_recv.at[s, h], (row, 2 * chip_to + core))
+
+    def own_along(way, chip_to, h):
+        source = fp.at[pl.ds(pl.multiple_of(h * piece, piece), piece)]
+        place = slab.at[chip, chunk(core, h)]
+        return remote(source, place, z_send.at[way, chip, h], z_recv.at[chip, h], (row, 2 * chip_to + core))
+
+    def to_twin(s, of, h):
+        place = slab.at[s, chunk(of, h)]
+        return remote(place, place, s_send.at[s, h], s_recv.at[s, h], (row, twin))
+
+    def own_to_twin(h):
+        source = fp.at[pl.ds(pl.multiple_of(h * piece, piece), piece)]
+        return remote(source, slab.at[chip, chunk(core, h)], s_send.at[chip, h], s_recv.at[chip, h], (row, twin))
 
     def rows_to(p):
         peer = flip(row, p, n_row)
@@ -77,20 +93,26 @@
     each(1, n_row, lambda p: greet((flip(row, p, n_row), col)))
     each(1, n_chip, lambda d: greet((row, 2 * ((chip + d) % n_chip) + core)))
     greet((row, twin))
-    slab[chip, mine] = fp[...]
-    cols[row] = fp[...]
-    cpr[row] = pr[...]
+    local = (
+        pltpu.make_async_copy(fp, slab.at[chip, mine], l_sem.at[0]),
+        pltpu.make_async_copy(fp, cols.at[row], l_sem.at[1]),
+        pltpu.make_async_copy(pr, cpr.at[row], l_sem.at[2]),
+    )
+    for copy in local:
+        copy.start()
+    part[...] = jnp.zeros_like(part)
     pl.semaphore_wait(barrier, n_row - 1 + n_chip - 1 + 1)
 
-    @pl.when(chip + 1 < n_chip)
-    def _():
-        along(chip, 0, chip + 1).start()
-
-    @pl.when(chip > 0)
-    def _():
-        along(chip, 1, chip - 1).start()
-
-    to_twin(chip, mine).start()
+    def start_own(h):
+        @pl.when(chip + 1 < n_chip)
+        def _():
+            own_along(0, chip + 1, h).start()
+
+        @pl.when(chip > 0)
+        def _():
+            own_along(1, chip - 1, h).start()
+    each(0, CHUNKS, start_own)
+    each(0, CHUNKS, lambda h: own_to_twin(h).start())
 
     def start_rows(p):
         for copy in rows_to(p):
@@ -111,30 +133,33 @@
         value = inner / (sq_first[s][:, :1] + sq_second[r][:1] - inner)
         part[s] += jnp.dot(value.astype(jnp.bfloat16), cpr[r], preferred_element_type=jnp.float32)
 
-    part[...] = jnp.zeros_like(part)
+    for copy in local:
+        copy.wait()
     prepare_second(row)
-    to_twin(chip, others).wait_recv()
+    each(0, CHUNKS, lambda h: to_twin(chip, 1 - core, h).wait_recv())
     prepare_first(chip)
     tile(chip, row)
 
     def receive(d, onward):
-        @pl.when(chip - d >= 0)
-        def _():
-            along(chip - d, 0, chip).wait_recv()
-            if onward:
-                @pl.when(chip + 1 < n_chip)
-                def _():
-                    along(chip - d, 0, chip + 1).start()
-            to_twin(chip - d, mine).start()
-
-        @pl.when(chip + d < n_chip)
-        def _():
-            along(chip + d, 1, chip).wait_recv()
-            if onward:
-                @pl.when(chip > 0)
-                def _():
-                    along(chip + d, 1, chip - 1).start()
-            to_twin(chip + d, mine).start()
+        def one(h):
+            @pl.when(chip - d >= 0)
+            def _():
+                along(chip - d, 0, chip, h).wait_recv()
+                if onward:
+                    @pl.when(chip + 1 < n_chip)
+                    def _():
+                        along(chip - d, 0, chip + 1, h).start()
+                to_twin(chip - d, core, h).start()
+
+            @pl.when(chip + d < n_chip)
+            def _():
+                along(chip + d, 1, chip, h).wait_recv()
+                if onward:
+                    @pl.when(chip > 0)
+                    def _():
+                        along(chip + d, 1, chip - 1, h).start()
+                to_twin(chip + d, core, h).start()
+        each(0, CHUNKS, one)
 
     def both_sides(d, body):
         def side(k):
@@ -146,7 +171,7 @@
         each(0, 2, side)
 
     def take(s):
-        to_twin(s, others).wait_recv()
+        each(0, CHUNKS, lambda h: to_twin(s, 1 - core, h).wait_recv())
         prepare_first(s)
 
     def middle(d):
@@ -205,16 +230,19 @@
     out[...] *= factor
 
     def sent(s):
-        to_twin(s, mine).wait_send()
         partial_to_twin(s).wait_send()
 
-        @pl.when((s <= chip) & (chip + 1 < n_chip))
-        def _():
-            along(s, 0, chip).wait_send()
-
-        @pl.when((s >= chip) & (chip > 0))
-        def _():
-            along(s, 1, chip).wait_send()
+        def pieces_sent(h):
+            to_twin(s, core, h).wait_send()
+
+            @pl.when((s <= chip) & (chip + 1 < n_chip))
+            def _():
+                along(s, 0, chip, h).wait_send()
+
+            @pl.when((s >= chip) & (chip > 0))
+            def _():
+                along(s, 1, chip, h).wait_send()
+        each(0, CHUNKS, pieces_sent)
 
         @pl.when(s != chip)
         def _():
@@ -236,7 +264,7 @@
     return pl.pallas_call(
         functools.partial(kernel, n_row, n_chip, factor),
         out_shape=jax.ShapeDtypeStruct((rows, width), jnp.float32),
-        in_specs=[pl.BlockSpec(memory_space=pltpu.VMEM)] * 2,
+        in_specs=[pl.BlockSpec(memory_space=pl.ANY)] * 2,
         out_specs=pl.BlockSpec(memory_space=pltpu.VMEM),
         scratch_shapes=[
             pltpu.VMEM((n_chip, 2 * rows, features), jnp.bfloat16),
@@ -248,15 +276,16 @@
             pltpu.VMEM((n_chip, rows, width), SENT),
             pltpu.VMEM((n_chip, 2 * rows, 128), jnp.float32),
             pltpu.VMEM((n_row, 8, rows), jnp.float32),
-            dma((2, n_chip)), dma((n_chip,)),
-            dma((n_chip,)), dma((n_chip,)),
+            dma((2, n_chip, CHUNKS)), dma((n_chip, CHUNKS)),
+            dma((n_chip, CHUNKS)), dma((n_chip, CHUNKS)),
             dma((n_row,)), dma((n_row,)),
             dma((n_row,)), dma((n_row,)),
             dma((n_chip,)), dma((n_chip,)),
             dma((n_chip,)), dma((n_chip,)),
+            dma((3,)),
         ],
         compiler_params=pltpu.CompilerParams(
-            collective_id=0, has_side_effects=True, vmem_limit_bytes=48 * 1024 * 1024
+            collective_id=0, has_side_effects=True, vmem_limit_bytes=62 * 1024 * 1024
         ),
     )(fingerprints, probes)
 

time: 67.1 us -> 55.3 us (0.82)
  the two profiles are of different devices: /device:TPU:24 before, /device:TPU:0 now
where the time goes in v2:
time: 55.3 us; the launch traced here: 55.2 us
  Pallas kernels  53.5 us (97%)
  local copies, waits for them, and re-layouts  1.67 us (3%)
    pallas_call x1, Pallas kernels, per_device(): pl.pallas_call(functools.partial(kernel, n_row, n_chip, factor), out_shap...  53.5 us
    unnamed x1, local copies, waits for them, and re-layouts  1.67 us

profile of v2, /device:TPU:0, one launch (start us, length us, event | category | flops | bytes accessed | tf_op | source)
XLA Modules:
  0.0 55.2 jit_solution(12815578736875507565)
XLA Ops:
  0.0 53.5 %shard_map.28 = f32[256,256]{1,0:T(8,128)} custom-call(bf16[256,1024]{1,0:T(8,128)(2,1)} %fp.1, bf16[256,256]{1,0:T(8,128)(2,1)} %pr.1), custom_call_target="tpu_custom_call" | custom-call | tf_op jit(solution)/shard_map/pallas_call | solution.py:264
  53.5 1.7 %copy.4 = f32[256,256]{1,0:T(8,128)} copy(f32[256,256]{1,0:T(8,128)} %shard_map.28) | data formatting | bytes 524288

commit v3 on v2

--- a/solution.py
+++ b/solution.py
@@ -11,6 +11,8 @@
 MESH = pl.DeviceIdType.MESH
 SENT = jnp.bfloat16
 CHUNKS = 2
+ONE_WAY = ((0, 1), (2, 1), (3, 1), (2, 0), (3, 0), (3, 2))
+ONE_WAY_CHIPS = 4
 
 
 def flip(index, pattern, size):
@@ -21,7 +23,15 @@
     return result
 
 
-def kernel(n_row, n_chip, factor, fp, pr, out, slab, cols, cpr, part, other, stage, ret, sq_first, sq_second,
+def any_of(pairs, s, t):
+    found = (s < 0) & (s > 0)
+    for a, b in pairs:
+        found = found | ((s == a) & (t == b))
+    return found
+
+
+def kernel(n_row, n_chip, factor, fp, pr, out, slab, cols, cpr, spr, part, other, stage, ret, extra, xstage, xin,
+           sq_first, sq_second, q_send, q_recv, t_send, t_recv, x_send, x_recv,
            z_send, z_recv, s_send, s_recv, f_send, f_recv, p_send, p_recv, o_send, o_recv, r_send, r_recv, l_sem):
     rows = fp.shape[0]
     row, col = lax.axis_index("row"), lax.axis_index("col")
@@ -31,6 +41,24 @@
     piece = rows // CHUNKS
     others = pl.ds(pl.multiple_of((1 - core) * rows, rows), rows)
 
+    one_way = ONE_WAY if n_chip == ONE_WAY_CHIPS else ()
+    probed = sorted({a for a, _ in one_way})
+    turned = sorted({b for _, b in one_way})
+
+    def goes(s, t):
+        return jnp.logical_not(any_of([(b, a) for a, b in one_way], s, t)) & (s != t)
+
+    def have(s):
+        return (s == chip) | goes(s, chip)
+
+    def twice(s):
+        return any_of(one_way, s, chip)
+
+    def with_probes(s):
+        return any_of([(a, 0) for a in probed], s, 0)
+
+    turns = any_of([(b, 0) for b in turned], chip, 0)
+
     def remote(src, dst, send, recv, where):
         return pltpu.make_async_remote_copy(
             src_ref=src, dst_ref=dst, send_sem=send, recv_sem=recv, device_id=where, device_id_type=MESH
@@ -47,6 +75,21 @@
         source = fp.at[pl.ds(pl.multiple_of(h * piece, piece), piece)]
         place = slab.at[chip, chunk(core, h)]
         return remote(source, place, z_send.at[way, chip, h], z_recv.at[chip, h], (row, 2 * chip_to + core))
+
+    def probes_along(s, way, chip_to):
+        place = spr.at[s, mine]
+        return remote(place, place, q_send.at[way, s], q_recv.at[s], (row, 2 * chip_to + core))
+
+    def own_probes_along(way, chip_to):
+        return remote(pr, spr.at[chip, mine], q_send.at[way, chip], q_recv.at[chip], (row, 2 * chip_to + core))
+
+    def probes_to_twin(s, half):
+        place = spr.at[s, half]
+        return remote(place, place, t_send.at[s], t_recv.at[s], (row, twin))
+
+    def extra_to(p):
+        peer = flip(row, p, n_row)
+        return remote(xstage.at[peer], xin.at[p], x_send.at[p], x_recv.at[p], (peer, col))
 
     def to_twin(s, of, h):
         place = slab.at[s, chunk(of, h)]
@@ -101,17 +144,27 @@
     for copy in local:
         copy.start()
     part[...] = jnp.zeros_like(part)
+    extra[...] = jnp.zeros_like(extra)
     pl.semaphore_wait(barrier, n_row - 1 + n_chip - 1 + 1)
 
     def start_own(h):
-        @pl.when(chip + 1 < n_chip)
+        @pl.when((chip + 1 < n_chip) & goes(chip, chip + 1))
         def _():
             own_along(0, chip + 1, h).start()
 
-        @pl.when(chip > 0)
+        @pl.when((chip > 0) & goes(chip, chip - 1))
         def _():
             own_along(1, chip - 1, h).start()
     each(0, CHUNKS, start_own)
+
+    if one_way:
+        @pl.when((chip + 1 < n_chip) & goes(chip, chip + 1) & with_probes(chip))
+        def _():
+            own_probes_along(0, chip + 1).start()
+
+        @pl.when((chip > 0) & goes(chip, chip - 1) & with_probes(chip))
+        def _():
+            own_probes_along(1, chip - 1).start()
     each(0, CHUNKS, lambda h: own_to_twin(h).start())
 
     def start_rows(p):
@@ -131,7 +184,14 @@
     def tile(s, r):
         inner = lax.dot_general(slab[s], cols[r], (((1,), (1,)), ((), ())), preferred_element_type=jnp.float32)
         value = inner / (sq_first[s][:, :1] + sq_second[r][:1] - inner)
-        part[s] += jnp.dot(value.astype(jnp.bfloat16), cpr[r], preferred_element_type=jnp.float32)
+        value = value.astype(jnp.bfloat16)
+        part[s] += jnp.dot(value, cpr[r], preferred_element_type=jnp.float32)
+        if one_way:
+            @pl.when(twice(s))
+            def _():
+                extra[r] += lax.dot_general(
+                    value, spr[s], (((0,), (0,)), ((), ())), preferred_element_type=jnp.float32
+                )
 
     for copy in local:
         copy.wait()
@@ -141,31 +201,34 @@
     tile(chip, row)
 
     def receive(d, onward):
-        def one(h):
-            @pl.when(chip - d >= 0)
-            def _():
-                along(chip - d, 0, chip, h).wait_recv()
-                if onward:
-                    @pl.when(chip + 1 < n_chip)
+        def moved(s, way, there, inside):
+            @pl.when((s >= 0) & (s < n_chip) & goes(s, chip))
+            def _():
+                def one(h):
+                    along(s, way, chip, h).wait_recv()
+                    if onward:
+                        @pl.when(inside & goes(s, there))
+                        def _():
+                            along(s, way, there, h).start()
+                    to_twin(s, core, h).start()
+                each(0, CHUNKS, one)
+                if one_way:
+                    @pl.when(with_probes(s))
                     def _():
-                        along(chip - d, 0, chip + 1, h).start()
-                to_twin(chip - d, core, h).start()
-
-            @pl.when(chip + d < n_chip)
-            def _():
-                along(chip + d, 1, chip, h).wait_recv()
-                if onward:
-                    @pl.when(chip > 0)
-                    def _():
-                        along(chip + d, 1, chip - 1, h).start()
-                to_twin(chip + d, core, h).start()
-        each(0, CHUNKS, one)
+                        probes_along(s, way, chip).wait_recv()
+                        if onward:
+                            @pl.when(inside & goes(s, there))
+                            def _():
+                                probes_along(s, way, there).start()
+                        probes_to_twin(s, mine).start()
+        moved(chip - d, 0, chip + 1, chip + 1 < n_chip)
+        moved(chip + d, 1, chip - 1, chip > 0)
 
     def both_sides(d, body):
         def side(k):
             s = chip + d * (2 * k - 1)
 
-            @pl.when((s >= 0) & (s < n_chip))
+            @pl.when((s >= 0) & (s < n_chip) & goes(s, chip))
             def _():
                 body(s)
         each(0, 2, side)
@@ -173,6 +236,10 @@
     def take(s):
         each(0, CHUNKS, lambda h: to_twin(s, 1 - core, h).wait_recv())
         prepare_first(s)
+        if one_way:
+            @pl.when(with_probes(s))
+            def _():
+                probes_to_twin(s, others).wait_recv()
 
     def middle(d):
         receive(d, True)
@@ -187,7 +254,7 @@
 
     def near(body):
         def check(s):
-            @pl.when((s - chip < last) & (chip - s < last))
+            @pl.when((s - chip < last) & (chip - s < last) & have(s))
             def _():
                 body(s)
         each(0, n_chip, check)
@@ -217,37 +284,77 @@
         take(s)
         each(0, n_row, lambda r: tile(s, r))
         partial_to_twin(s).start()
-        hand_on(s)
     both_sides(last, far)
 
+    if one_way:
+        def extra_start(p):
+            peer = flip(row, p, n_row)
+            xstage[peer] = extra[peer].astype(SENT)
+            extra_to(p).start()
+
+        @pl.when(turns)
+        def _():
+            each(1, n_row, extra_start)
+    both_sides(last, hand_on)
+
     out[...] = part[chip, mine] + other[chip]
+
+    if one_way:
+        def extra_add(p):
+            extra_to(p).wait_recv()
+            out[...] += xin[p].astype(jnp.float32)
+
+        @pl.when(turns)
+        def _():
+            out[...] += extra[row]
+            each(1, n_row, extra_add)
 
     def add(d):
         s = (chip + d) % n_chip
-        result_from(s).wait_recv()
-        out[...] += ret[s].astype(jnp.float32)
+
+        @pl.when(goes(chip, s))
+        def _():
+            result_from(s).wait_recv()
+            out[...] += ret[s].astype(jnp.float32)
     each(1, n_chip, add)
     out[...] *= factor
 
+    def left(s, way):
+        def pieces(h):
+            along(s, way, chip, h).wait_send()
+        each(0, CHUNKS, pieces)
+        if one_way:
+            @pl.when(with_probes(s))
+            def _():
+                probes_along(s, way, chip).wait_send()
+
     def sent(s):
-        partial_to_twin(s).wait_send()
-
-        def pieces_sent(h):
-            to_twin(s, core, h).wait_send()
-
-            @pl.when((s <= chip) & (chip + 1 < n_chip))
-            def _():
-                along(s, 0, chip, h).wait_send()
-
-            @pl.when((s >= chip) & (chip > 0))
-            def _():
-                along(s, 1, chip, h).wait_send()
-        each(0, CHUNKS, pieces_sent)
-
-        @pl.when(s != chip)
-        def _():
-            result_to(s).wait_send()
+        @pl.when(have(s))
+        def _():
+            partial_to_twin(s).wait_send()
+            each(0, CHUNKS, lambda h: to_twin(s, core, h).wait_send())
+            if one_way:
+                @pl.when(with_probes(s) & (s != chip))
+                def _():
+                    probes_to_twin(s, mine).wait_send()
+
+            @pl.when((s <= chip) & (chip + 1 < n_chip) & goes(s, chip + 1))
+            def _():
+                left(s, 0)
+
+            @pl.when((s >= chip) & (chip > 0) & goes(s, chip - 1))
+            def _():
+                left(s, 1)
+
+            @pl.when(s != chip)
+            def _():
+                result_to(s).wait_send()
     each(0, n_chip, sent)
+
+    if one_way:
+        @pl.when(turns)
+        def _():
+            each(1, n_row, lambda p: extra_to(p).wait_send())
 
     def rows_sent(p):
         for copy in rows_to(p):
@@ -270,12 +377,19 @@
             pltpu.VMEM((n_chip, 2 * rows, features), jnp.bfloat16),
             pltpu.VMEM((n_row, rows, features), jnp.bfloat16),
             pltpu.VMEM((n_row, rows, width), jnp.bfloat16),
+            pltpu.VMEM((n_chip, 2 * rows, width), jnp.bfloat16),
             pltpu.VMEM((n_chip, 2 * rows, width), jnp.float32),
             pltpu.VMEM((n_chip, rows, width), jnp.float32),
             pltpu.VMEM((n_chip, rows, width), SENT),
             pltpu.VMEM((n_chip, rows, width), SENT),
+            pltpu.VMEM((n_row, rows, width), jnp.float32),
+            pltpu.VMEM((n_row, rows, width), SENT),
+            pltpu.VMEM((n_row, rows, width), SENT),
             pltpu.VMEM((n_chip, 2 * rows, 128), jnp.float32),
             pltpu.VMEM((n_row, 8, rows), jnp.float32),
+            dma((2, n_chip)), dma((n_chip,)),
+            dma((n_chip,)), dma((n_chip,)),
+            dma((n_row,)), dma((n_row,)),
             dma((2, n_chip, CHUNKS)), dma((n_chip, CHUNKS)),
             dma((n_chip, CHUNKS)), dma((n_chip, CHUNKS)),
             dma((n_row,)), dma((n_row,)),

time: 55.3 us -> 66.9 us (1.21)
  Pallas kernels: 53.5 us -> 65 us
    pallas_call x1, Pallas kernels: 53.5 us -> 65 us  [per_device(): pl.pallas_call(functools.partial(kernel, n_row, n_chip, factor), out_shap...]
where the time goes in v3:
time: 66.9 us; the launch traced here: 66.7 us
  Pallas kernels  65 us (97%)
  local copies, waits for them, and re-layouts  1.67 us (2%)
    pallas_call x1, Pallas kernels, per_device(): pl.pallas_call(functools.partial(kernel, n_row, n_chip, factor), out_shap...  65 us
    unnamed x1, local copies, waits for them, and re-layouts  1.67 us

profile of v3, /device:TPU:0, one launch (start us, length us, event | category | flops | bytes accessed | tf_op | source)
XLA Modules:
  0.0 66.7 jit_solution(11648211524912346650)
XLA Ops:
  0.0 65.0 %shard_map.28 = f32[256,256]{1,0:T(8,128)} custom-call(bf16[256,1024]{1,0:T(8,128)(2,1)} %fp.1, bf16[256,256]{1,0:T(8,128)(2,1)} %pr.1), custom_call_target="tpu_custom_call" | custom-call | tf_op jit(solution)/shard_map/pallas_call | solution.py:371
  65.0 1.7 %copy.4 = f32[256,256]{1,0:T(8,128)} copy(f32[256,256]{1,0:T(8,128)} %shard_map.28) | data formatting | bytes 524288

commit v4 on v2

--- a/solution.py
+++ b/solution.py
@@ -197,7 +197,17 @@
             copy.wait_recv()
         peer = flip(row, p, n_row)
         prepare_second(peer)
-        near(lambda s: tile(s, peer))
+
+        @pl.when(p < n_row - 1)
+        def _():
+            near(lambda s: tile(s, peer))
+
+        @pl.when(p == n_row - 1)
+        def _():
+            def finish(s):
+                tile(s, peer)
+                partial_to_twin(s).start()
+            near(finish)
     each(1, n_row, row_step)
 
     def hand_on(s):
@@ -208,7 +218,6 @@
             stage[s] = (part[s, mine] + other[s]).astype(SENT)
             result_to(s).start()
 
-    near(lambda s: partial_to_twin(s).start())
     near(hand_on)
 
     receive(last, False)

time: 55.3 us -> 54.5 us (0.986)
  Pallas kernels: 53.5 us -> 52.7 us
    pallas_call x1, Pallas kernels: 53.5 us -> 52.7 us  [per_device(): pl.pallas_call(functools.partial(kernel, n_row, n_chip, factor), out_shap...]
where the time goes in v4:
time: 54.5 us; the launch traced here: 54.4 us
  Pallas kernels  52.7 us (97%)
  local copies, waits for them, and re-layouts  1.67 us (3%)
    pallas_call x1, Pallas kernels, per_device(): pl.pallas_call(functools.partial(kernel, n_row, n_chip, factor), out_shap...  52.7 us
    unnamed x1, local copies, waits for them, and re-layouts  1.67 us

profile of v4, /device:TPU:0, one launch (start us, length us, event | category | flops | bytes accessed | tf_op | source)
XLA Modules:
  0.0 54.4 jit_solution(16723296868093664286)
XLA Ops:
  0.0 52.7 %shard_map.28 = f32[256,256]{1,0:T(8,128)} custom-call(bf16[256,1024]{1,0:T(8,128)(2,1)} %fp.1, bf16[256,256]{1,0:T(8,128)(2,1)} %pr.1), custom_call_target="tpu_custom_call" | custom-call | tf_op jit(solution)/shard_map/pallas_call | solution.py:273
  52.7 1.7 %copy.4 = f32[256,256]{1,0:T(8,128)} copy(f32[256,256]{1,0:T(8,128)} %shard_map.28) | data formatting | bytes 524288

commit v5 on v4

--- a/solution.py
+++ b/solution.py
@@ -117,7 +117,9 @@
     def start_rows(p):
         for copy in rows_to(p):
             copy.start()
-    each(1, n_row, start_rows)
+    each(1, n_row - 1, start_rows)
+    if n_chip < 3:
+        start_rows(n_row - 1)
 
     def prepare_first(s):
         values = slab[s].astype(jnp.float32)
@@ -176,6 +178,10 @@
 
     def middle(d):
         receive(d, True)
+
+        @pl.when(d == 1)
+        def _():
+            start_rows(n_row - 1)
 
         def body(s):
             take(s)

time: 54.5 us -> 54.5 us (level)
  no operation moved by 1% of the time
where the time goes in v5:
time: 54.5 us; the launch traced here: 54.4 us
  Pallas kernels  52.7 us (97%)
  local copies, waits for them, and re-layouts  1.67 us (3%)
    pallas_call x1, Pallas kernels, per_device(): pl.pallas_call(functools.partial(kernel, n_row, n_chip, factor), out_shap...  52.7 us
    unnamed x1, local copies, waits for them, and re-layouts  1.67 us

profile of v5, /device:TPU:0, one launch (start us, length us, event | category | flops | bytes accessed | tf_op | source)
XLA Modules:
  0.0 54.4 jit_solution(11720328119443817141)
XLA Ops:
  0.0 52.7 %shard_map.28 = f32[256,256]{1,0:T(8,128)} custom-call(bf16[256,1024]{1,0:T(8,128)(2,1)} %fp.1, bf16[256,256]{1,0:T(8,128)(2,1)} %pr.1), custom_call_target="tpu_custom_call" | custom-call | tf_op jit(solution)/shard_map/pallas_call | solution.py:279
  52.7 1.7 %copy.4 = f32[256,256]{1,0:T(8,128)} copy(f32[256,256]{1,0:T(8,128)} %shard_map.28) | data formatting | bytes 524288
